TPU v7x, 32 devices: a whole 2x2x4 slice. The times are simulated.
32 devices in a mesh: space: 8 (over z, y), chan: 4 (over x, core).
Axes of the slice: x: 2, y: 2, z: 4, core: 2. Of those that a mesh axis runs over, the one named last changes fastest.
Arguments:
- volume: bfloat16 [16, 32, 128, 128], P(None, 'space', 'chan'), may hold values from -6 to 6
- kernel: bfloat16 [27, 128, 128], P(None, None, 'chan'), may hold values from -0.109375 to 0.109375
- bias: float32 [128], P('chan'), may hold values from -3 to 3
- cotangent: bfloat16 [16, 32, 128, 128], P(None, 'space', 'chan'), may hold values from -6 to 6
Outputs:
- output: bfloat16 [16, 32, 128, 128], P(None, 'space', 'chan')
- volume_grad: bfloat16 [16, 32, 128, 128], P(None, 'space', 'chan')
All inputs are finite; a program needn't handle non-finite values.
Results may differ from a plain program's by a relative error of at most 0.001.
Values may be sent and summed in bfloat16 or wider, within the bound.
A program may use at most 128 MiB of HBM per device.

v0:
```python
import jax
import jax.numpy as jnp
from jax import lax
from jax.sharding import PartitionSpec as P


def with_halo(block, sides, width):
    for axis, dim in sides:
        count = lax.axis_size(axis)
        forward = [(i, i + 1) for i in range(count - 1)]
        backward = [(target, source) for source, target in forward]
        low = lax.ppermute(
            lax.slice_in_dim(block, block.shape[dim] - width, None, axis=dim), axis, forward
        )
        high = lax.ppermute(lax.slice_in_dim(block, 0, width, axis=dim), axis, backward)
        block = jnp.concatenate([low, block, high], axis=dim)
    return block


def shifted_terms(padded, weights, forward, total):
    planes = padded.shape[0] - 2
    rows = padded.shape[1] - 2
    columns = padded.shape[3] - 2
    channels = padded.shape[2]
    group = 9 if channels < 128 else 1
    for first in range(0, 27, group):
        windows = []
        weight_list = []
        for offset in range(first, first + group):
            steps_at = (offset // 9, offset // 3 % 3, offset % 3)
            if not forward:
                steps_at = (2 - steps_at[0], 2 - steps_at[1], 2 - steps_at[2])
            windows.append(
                padded[
                    steps_at[0] : steps_at[0] + planes,
                    steps_at[1] : steps_at[1] + rows,
                    :,
                    steps_at[2] : steps_at[2] + columns,
                ]
            )
            weight_list.append(weights[offset])
        if group == 1:
            stacked = windows[0]
        else:
            stacked = jnp.concatenate(windows, axis=2)
        if forward:
            weight_now = weight_list[0]
            total = total + jnp.einsum(
                "xyiz,io->xyoz", stacked, weight_now, preferred_element_type=jnp.float32
            )
        else:
            weight_now = jnp.concatenate(weight_list, axis=1)
            total = total + jnp.einsum(
                "xyoz,io->xyiz", stacked, weight_now, preferred_element_type=jnp.float32
            )
    return total


def pad_sides(field):
    return jnp.pad(field, ((1, 1), (0, 0), (0, 0), (1, 1)))


def per_device(volume, kernel, bias, cotangent):
    start_sum = jnp.zeros(volume.shape, jnp.float32) + bias[None, None, :, None]
    whole = lax.all_gather(volume, "chan", axis=2, tiled=True)
    with_rows = with_halo(whole, (("space", 1),), 1)
    forward_sum = shifted_terms(pad_sides(with_rows), kernel, True, start_sum)
    output = forward_sum.astype(jnp.bfloat16)
    grad_rows = with_halo(cotangent, (("space", 1),), 1)
    empty = jnp.zeros(
        (volume.shape[0], volume.shape[1], kernel.shape[1], volume.shape[3]), jnp.float32
    )
    partials = shifted_terms(pad_sides(grad_rows), kernel, False, empty)
    volume_grad = lax.psum_scatter(partials, "chan", scatter_dimension=2, tiled=True)
    return (output, volume_grad.astype(jnp.bfloat16))


def solution(mesh):
    return jax.shard_map(
        per_device,
        mesh=mesh,
        in_specs=(
            P(None, "space", "chan", None),
            P(None, None, "chan"),
            P("chan"),
            P(None, "space", "chan", None),
        ),
        out_specs=(P(None, "space", "chan", None), P(None, "space", "chan", None)),
        check_vma=False,
    )
```

profile of v0, /device:TPU:1, one launch (start us, length us, event | category | flops | bytes accessed | tf_op | source)
XLA Modules:
  0.0 109.8 jit_solution(14382280939171236170)
XLA Ops:
  7.2 1.0 fusion.247
  8.2 4.0 %collective-permute-start.2 = (bf16[16,1,32,128]{3,2,1,0:T(8,128)(2,1)S(1)}, bf16[16,1,32,128]{3,2,1,0:T(8,128)(2,1)S(1)}, u32[]{:S(2)}, u32[]{:S(2)}) collective-permute-start(bf16[16,1,32,128]{3,2,1,0:T(8,128)(2,1)S(1)} %get-tuple-element.26), channel_id=1, source_target_pairs={{0,4},{4,8},{8,12},{12,16},{16,20},{20,24},{24,28},{1,5},{5,9},{9,... | collective-permute-start | bytes 393224 | tf_op jit(solution)/shard_map/ppermute | solution.py:12
  12.2 1.3 %collective-permute-start.3 = (bf16[16,1,32,128]{3,2,1,0:T(8,128)(2,1)S(1)}, bf16[16,1,32,128]{3,2,1,0:T(8,128)(2,1)S(1)}, u32[]{:S(2)}, u32[]{:S(2)}) collective-permute-start(bf16[16,1,32,128]{3,2,1,0:T(8,128)(2,1)S(1)} %get-tuple-element.27), channel_id=1, source_target_pairs={{4,0},{8,4},{12,8},{16,12},{20,16},{24,20},{28,24},{5,1},{9,5},{13... | collective-permute-start | bytes 393224 | tf_op jit(solution)/shard_map/ppermute | solution.py:15
  13.6 0.7 constant_dynamic-update-slice_fusion.17
  14.3 0.7 constant_dynamic-update-slice_fusion.16
  15.0 0.8 constant_dynamic-update-slice_fusion.15
  15.8 0.7 constant_dynamic-update-slice_fusion.14
  16.5 0.7 constant_dynamic-update-slice_fusion.13
  17.2 0.7 constant_dynamic-update-slice_fusion.12
  18.0 0.7 constant_dynamic-update-slice_fusion.11
  18.7 0.7 constant_dynamic-update-slice_fusion.10
  19.5 0.7 constant_dynamic-update-slice_fusion.9
  20.2 0.7 constant_dynamic-update-slice_fusion.20
  20.9 0.7 constant_dynamic-update-slice_fusion.19
  21.6 2.0 %select_maximum_fusion.2 = bf16[18,6,32,130]{3,2,1,0:T(8,128)(2,1)S(1)} fusion(bf16[16,1,32,128]{3,2,1,0:T(8,128)(2,1)S(1)} %collective-permute-done.3, bf16[16,4,32,128]{3,2,1,0:T(8,128)(2,1)} %param.7, bf16[16,1,32,128]{3,2,1,0:T(8,128)(2,1)S(1)} %collective-permute-done.2), kind=kLoop, calls=%fused_computation.74 | loop fusion | flops 8536320 | bytes 1684992 | tf_op jit(solution)/shard_map/concatenate | solution.py:16
  23.7 0.2 slice_dynamic-update-slice_fusion.23
  23.9 0.5 slice_dynamic-update-slice_fusion.22
  24.4 0.5 slice_dynamic-update-slice_fusion.21
  24.9 0.6 slice_dynamic-update-slice_fusion.14
  25.6 0.7 slice_dynamic-update-slice_fusion.13
  26.3 0.7 slice_dynamic-update-slice_fusion.12
  27.2 0.6 slice_dynamic-update-slice_fusion.11
  27.8 0.9 slice_dynamic-update-slice_fusion.10
  28.8 0.6 slice_dynamic-update-slice_fusion.9
  29.4 0.1 slice_dynamic-update-slice_fusion
  29.6 3.3 %fusion.187 = f32[128,16,4,128]{3,0,2,1:T(8,128)} fusion(bf16[16,4,288,128]{3,2,1,0:T(8,128)(2,1)S(1)} %get-tuple-element.6, bf16[128,288]{0,1:T(8,128)(2,1)S(1)} %get-tuple-element.30), kind=kOutput, calls=%fused_computation.178 | convolution fusion | flops 603979776 | bytes 8986624 | tf_op jit(solution)/shard_map/xyoz,io->xyiz/dot_general | solution.py:53
  32.9 3.4 %fusion.184 = f32[128,16,4,128]{3,0,2,1:T(8,128)} fusion(bf16[16,4,288,128]{3,2,1,0:T(8,128)(2,1)S(1)} %slice_dynamic-update-slice_fusion, bf16[128,288]{0,1:T(8,128)(2,1)S(1)} %constant_dynamic-update-slice_fusion.19), kind=kOutput, calls=%fused_computation.175 | convolution fusion | flops 603979776 | bytes 8986624 | tf_op jit(solution)/shard_map/xyoz,io->xyiz/dot_general | solution.py:53
  36.3 3.0 %all-gather.2.cloned.1.call-done = bf16[16,4,128,128]{3,2,1,0:T(8,128)(2,1)} async-done(((bf16[16,4,32,128]{3,2,1,0:T(8,128)(2,1)}), bf16[16,4,128,128]{3,2,1,0:T(8,128)(2,1)}) %all-gather.2.cloned.1.call-update) | async-done | bytes 2097168 | tf_op jit(solution)/shard_map/all_gather | solution.py:65
  39.3 2.3 %fusion.246 = (bf16[16,1,128,128]{3,2,1,0:T(8,128)(2,1)}, bf16[16,1,128,128]{3,2,1,0:T(8,128)(2,1)}) fusion(bf16[16,4,128,128]{3,2,1,0:T(8,128)(2,1)} %all-gather.2.cloned.1.call-done), kind=kLoop, calls=%fused_computation.237 | loop fusion | bytes 2097152 | tf_op jit(solution)/shard_map/slice | solution.py:13
  41.6 3.1 %collective-permute-start = (bf16[16,1,128,128]{3,2,1,0:T(8,128)(2,1)}, bf16[16,1,128,128]{3,2,1,0:T(8,128)(2,1)S(1)}, u32[]{:S(2)}, u32[]{:S(2)}) collective-permute-start(bf16[16,1,128,128]{3,2,1,0:T(8,128)(2,1)} %get-tuple-element.2), channel_id=1, source_target_pairs={{0,4},{4,8},{8,12},{12,16},{16,20},{20,24},{24,28},{1,5},{5,9},{9,... | collective-permute-start | bytes 1572872 | tf_op jit(solution)/shard_map/ppermute | solution.py:12
  44.7 1.3 %collective-permute-start.1 = (bf16[16,1,128,128]{3,2,1,0:T(8,128)(2,1)}, bf16[16,1,128,128]{3,2,1,0:T(8,128)(2,1)S(1)}, u32[]{:S(2)}, u32[]{:S(2)}) collective-permute-start(bf16[16,1,128,128]{3,2,1,0:T(8,128)(2,1)} %get-tuple-element.3), channel_id=1, source_target_pairs={{4,0},{8,4},{12,8},{16,12},{20,16},{24,20},{28,24},{5,1},{9,5},{13... | collective-permute-start | bytes 1572872 | tf_op jit(solution)/shard_map/ppermute | solution.py:15
  46.0 8.2 %add_bitcast_fusion = f32[16,4,128,128]{3,2,1,0:T(8,128)} fusion(f32[128,16,4,128]{3,0,2,1:T(8,128)} %fusion.184, f32[128,16,4,128]{3,0,2,1:T(8,128)} %fusion.187, bf16[16,4,288,128]{3,2,1,0:T(8,128)(2,1)} %copy-done.2, bf16[128,288]{0,1:T(8,128)(2,1)S(1)} %get-tuple-element.28), kind=kOutput, calls=%fused_computation.16 | convolution fusion | flops 606076928 | bytes 17375232 | tf_op jit(solution)/shard_map/xyoz,io->xyiz/dot_general | solution.py:53
  54.3 1.6 %copy-done = bf16[16,4,128,128]{3,2,1,0:T(8,128)(2,1)S(1)} copy-done((bf16[16,4,128,128]{3,2,1,0:T(8,128)(2,1)S(1)}, bf16[16,4,128,128]{3,2,1,0:T(8,128)(2,1)}, u32[]{:S(2)}) %copy-start) | copy-done | bytes 2097176
  55.8 0.4 fusion.202
  56.2 11.0 %collective-permute-done = bf16[16,1,128,128]{3,2,1,0:T(8,128)(2,1)S(1)} collective-permute-done((bf16[16,1,128,128]{3,2,1,0:T(8,128)(2,1)}, bf16[16,1,128,128]{3,2,1,0:T(8,128)(2,1)S(1)}, u32[]{:S(2)}, u32[]{:S(2)}) %collective-permute-start) | collective-permute-done | bytes 524320 | tf_op jit(solution)/shard_map/ppermute | solution.py:12
  67.3 4.2 %select_maximum_fusion = bf16[18,6,128,130]{3,2,1,0:T(8,128)(2,1)S(1)} fusion(bf16[16,1,128,128]{3,2,1,0:T(8,128)(2,1)S(1)} %collective-permute-done.1, bf16[16,4,128,128]{3,2,1,0:T(8,128)(2,1)S(1)} %copy-done, bf16[16,1,128,128]{3,2,1,0:T(8,128)(2,1)S(1)} %collective-permute-done), kind=kLoop, calls=%fused_computation.7 | loop fusion | flops 34145280 | bytes 6739968 | tf_op jit(solution)/shard_map/concatenate | solution.py:16
  71.5 0.4 fusion.39
  71.9 0.4 fusion.79
  72.4 0.4 fusion.35
  72.8 0.9 fusion.37
  73.6 0.4 fusion.41
  74.1 0.9 fusion.43
  74.9 0.9 fusion.45
  75.8 0.4 fusion.47
  76.2 0.9 fusion.49
  77.1 0.9 fusion.51
  78.0 0.4 fusion.53
  78.4 0.9 fusion.55
  79.3 0.9 fusion.57
  80.1 0.4 fusion.101
  80.6 0.9 fusion.104
  81.4 0.9 fusion.107
  82.3 0.4 fusion.31
  82.7 0.9 fusion.80
  83.6 0.4 fusion.83
  84.0 0.9 fusion.86
  84.9 1.1 fusion.89
  86.0 0.4 fusion.92
  86.4 0.9 fusion.95
  87.3 0.9 fusion.98
  88.2 1.5 %fusion.161 = f32[16,4,128,32]{2,3,1,0:T(8,128)S(1)} fusion(f32[16,4,128,32]{2,3,1,0:T(8,128)S(1)} %fusion.202, f32[16,4,128,32]{2,3,1,0:T(8,128)S(1)} %fusion.35, f32[16,4,128,32]{2,3,1,0:T(8,128)S(1)} %fusion.37, f32[16,4,128,32]{2,3,1,0:T(8,128)S(1)} %fusion.39, f32[16,4,128,32]{2,3,1,0:T(8,128)S(1)} %fusion.41, f32[16,4,128,32]{2,3,1,0:T(8,128)S(1)} %fusion.43, ...), kind=kOutput, calls=%fused_computation.112 | convolution fusion | flops 70778880 | bytes 16785920 | tf_op jit(solution)/shard_map/xyiz,io->xyoz/dot_general | solution.py:48
  89.7 2.3 %fusion.179 = bf16[16,4,32,128]{3,2,1,0:T(8,128)(2,1)} fusion(f32[16,4,32,128]{3,2,1,0:T(8,128)S(1)} %fusion.107, f32[16,4,32,128]{3,2,1,0:T(8,128)S(1)} %fusion.104, f32[16,4,32,128]{3,2,1,0:T(8,128)S(1)} %fusion.101, f32[16,4,32,128]{3,2,1,0:T(8,128)S(1)} %fusion.98, f32[16,4,32,128]{3,2,1,0:T(8,128)S(1)} %fusion.95, f32[16,4,32,128]{3,2,1,0:T(8,128)S(1)} %fusion.92, ...), kind=kOutput, calls=%fused_computation.118 | convolution fusion | flops 70778880 | bytes 16261120 | tf_op jit(solution)/shard_map/xyiz,io->xyoz/dot_general | solution.py:48
  92.0 8.9 %reduce-scatter.2.cloned.1.call-done = f32[16,4,32,128]{3,2,1,0:T(8,128)} async-done(((f32[16,4,128,128]{3,2,1,0:T(8,128)}), f32[16,4,32,128]{3,2,1,0:T(8,128)}) %reduce-scatter.2.cloned.1.call-update) | async-done | bytes 1048592 | tf_op jit(solution)/shard_map/reduce_scatter | solution.py:74
  100.9 2.1 %convert_element_type.11 = bf16[16,4,32,128]{3,2,1,0:T(8,128)(2,1)} convert(f32[16,4,32,128]{3,2,1,0:T(8,128)} %reduce-scatter.2.cloned.1.call-done) | non-fusion elementwise | flops 262144 | bytes 1572864 | tf_op jit(solution)/shard_map/convert_element_type | solution.py:75
  (19 shorter events, 0.4 us)
Async XLA Ops:
  7.2 32.2 %all-gather.2.cloned.1.call-start = ((), (), s32[]{:S(2)}) async-start(), calls=%async_computation.1 | async-start | bytes 2621440 | tf_op jit(solution)/shard_map/all_gather | solution.py:65
  8.2 13.4 %collective-permute-start.2 = (bf16[16,1,32,128]{3,2,1,0:T(8,128)(2,1)S(1)}, bf16[16,1,32,128]{3,2,1,0:T(8,128)(2,1)S(1)}, u32[]{:S(2)}, u32[]{:S(2)}) collective-permute-start(bf16[16,1,32,128]{3,2,1,0:T(8,128)(2,1)S(1)} %get-tuple-element.26), channel_id=1, source_target_pairs={{0,4},{4,8},{8,12},{12,16},{16,20},{20,24},{24,28},{1,5},{5,9},{9,... | collective-permute-start | bytes 393224 | tf_op jit(solution)/shard_map/ppermute | solution.py:12
  12.2 9.4 %collective-permute-start.3 = (bf16[16,1,32,128]{3,2,1,0:T(8,128)(2,1)S(1)}, bf16[16,1,32,128]{3,2,1,0:T(8,128)(2,1)S(1)}, u32[]{:S(2)}, u32[]{:S(2)}) collective-permute-start(bf16[16,1,32,128]{3,2,1,0:T(8,128)(2,1)S(1)} %get-tuple-element.27), channel_id=1, source_target_pairs={{4,0},{8,4},{12,8},{16,12},{20,16},{24,20},{28,24},{5,1},{9,5},{13... | collective-permute-start | bytes 393224 | tf_op jit(solution)/shard_map/ppermute | solution.py:15
  13.5 87.3 %reduce-scatter.2.cloned.1.call-start = ((), (), s32[]{:S(2)}) async-start(), calls=%async_computation.2 | async-start | bytes 5242880 | tf_op jit(solution)/shard_map/reduce_scatter | solution.py:74
  23.6 1.8 %copy-start.1 = (bf16[16,4,32,128]{3,2,1,0:T(8,128)(2,1)S(1)}, bf16[16,4,32,128]{3,2,1,0:T(8,128)(2,1)}, u32[]{:S(2)}) copy-start(bf16[16,4,32,128]{3,2,1,0:T(8,128)(2,1)} %param.7) | copy-start | bytes 1572868
  29.4 3.5 %copy-start.2 = (bf16[16,4,288,128]{3,2,1,0:T(8,128)(2,1)}, bf16[16,4,288,128]{3,2,1,0:T(8,128)(2,1)S(1)}, u32[]{:S(2)}) copy-start(bf16[16,4,288,128]{3,2,1,0:T(8,128)(2,1)S(1)} %get-tuple-element.4) | copy-start | bytes 14155780
  41.6 25.7 %collective-permute-start = (bf16[16,1,128,128]{3,2,1,0:T(8,128)(2,1)}, bf16[16,1,128,128]{3,2,1,0:T(8,128)(2,1)S(1)}, u32[]{:S(2)}, u32[]{:S(2)}) collective-permute-start(bf16[16,1,128,128]{3,2,1,0:T(8,128)(2,1)} %get-tuple-element.2), channel_id=1, source_target_pairs={{0,4},{4,8},{8,12},{12,16},{16,20},{20,24},{24,28},{1,5},{5,9},{9,... | collective-permute-start | bytes 1572872 | tf_op jit(solution)/shard_map/ppermute | solution.py:12
  44.7 22.6 %collective-permute-start.1 = (bf16[16,1,128,128]{3,2,1,0:T(8,128)(2,1)}, bf16[16,1,128,128]{3,2,1,0:T(8,128)(2,1)S(1)}, u32[]{:S(2)}, u32[]{:S(2)}) collective-permute-start(bf16[16,1,128,128]{3,2,1,0:T(8,128)(2,1)} %get-tuple-element.3), channel_id=1, source_target_pairs={{4,0},{8,4},{12,8},{16,12},{20,16},{24,20},{28,24},{5,1},{9,5},{13... | collective-permute-start | bytes 1572872 | tf_op jit(solution)/shard_map/ppermute | solution.py:15
  46.0 8.3 %copy-start.3 = (bf16[27,128,32]{1,2,0:T(8,128)(2,1)S(1)}, bf16[27,128,32]{1,2,0:T(8,128)(2,1)}, u32[]{:S(2)}) copy-start(bf16[27,128,32]{1,2,0:T(8,128)(2,1)} %param.5) | copy-start | bytes 663556
  54.2 1.6 %copy-start = (bf16[16,4,128,128]{3,2,1,0:T(8,128)(2,1)S(1)}, bf16[16,4,128,128]{3,2,1,0:T(8,128)(2,1)}, u32[]{:S(2)}) copy-start(bf16[16,4,128,128]{3,2,1,0:T(8,128)(2,1)} %all-gather.2.cloned.1.call-done) | copy-start | bytes 6291460
  86.0 2.2 %copy-start.4 = (f32[32]{0:T(128)S(1)}, f32[32]{0:T(128)}, u32[]{:S(2)}) copy-start(f32[32]{0:T(128)} %param.6) | copy-start | bytes 388
Sparse Core Ops, SparseCore 0:
  13.6 25.6 all-gather.1
  54.4 46.4 reduce-scatter.1
where the time goes:
time: 112 us; the launch traced here: 110 us
  matrix products  35.7 us (32%)
  waiting for transfers between devices  23 us (21%)
  local copies, waits for them, and re-layouts  18.5 us (17%)
  between operations  14.3 us (13%)
  starting transfers between devices  9.76 us (9%)
  other arithmetic  8.57 us (8%)
    dot_general x27, matrix products, shifted_terms(): jnp.einsum('xyiz,io->xyoz', stacked, weight_now, preferred_element_type=j...  20.8 us
    dot_general x3, matrix products, shifted_terms(): jnp.einsum('xyoz,io->xyiz', stacked, weight_now, preferred_element_type=j...  14.9 us
    unnamed x28, local copies, waits for them, and re-layouts  13.1 us
    ppermute x2, waiting for transfers between devices, with_halo(): lax.ppermute(lax.slice_in_dim(block, block.shape[dim] - width, None, axis...  11 us
    reduce_scatter x1, waiting for transfers between devices, per_device(): lax.psum_scatter(partials, 'chan', scatter_dimension=2, tiled=True)  8.9 us
    ppermute x2, starting transfers between devices, with_halo(): lax.ppermute(lax.slice_in_dim(block, block.shape[dim] - width, None, axis...  7.1 us
    concatenate x2, other arithmetic, with_halo(): block = jnp.concatenate([low, block, high], axis=dim)  6.27 us
    slice x2, local copies, waits for them, and re-layouts, with_halo(): lax.slice_in_dim(block, block.shape[dim] - width, None, axis=dim)  3.28 us
  transfers between devices with their start and end apart: 6, of which 3 were waited for; matrix products, arithmetic and copies ran while one was open for 51% of the time, Pallas kernels for 0%

commit v1 on v0

v1 whole, which is shorter than its diff:
```python
import functools

import jax
import jax.numpy as jnp
from jax import lax
from jax.experimental import pallas as pl
from jax.experimental.pallas import tpu as pltpu
from jax.sharding import PartitionSpec as P

MESH = pl.DeviceIdType.MESH


def convolve(padded, weights, start, out, first, last):
    rows = padded.shape[1] - 2
    channels, cells = padded.shape[2], padded.shape[3]
    block = weights.shape[0] // 3

    def plane(p, carry):
        total = None
        for a in range(3):
            right = jnp.concatenate(
                [
                    padded[p + a, r : r + 3].reshape(3 * channels, cells)
                    for r in range(rows)
                ],
                axis=1,
            )
            part = jnp.dot(
                weights[:, a * 3 * channels : (a + 1) * 3 * channels],
                right,
                preferred_element_type=jnp.float32,
            )
            total = part if total is None else total + part
        lane = lax.broadcasted_iota(jnp.int32, (block, cells), 1)
        for r in range(rows):
            piece = total[:, r * cells : (r + 1) * cells]
            low = pltpu.roll(piece[:block], 1, 1)
            high = pltpu.roll(piece[2 * block :], cells - 1, 1)
            result = piece[block : 2 * block]
            result = result + jnp.where(lane == 0, 0.0, low)
            result = result + jnp.where(lane == cells - 1, 0.0, high)
            if start is not None:
                result = result + start[...]
            out[p, r] = result.astype(out.dtype)
        return carry

    lax.fori_loop(first, last, plane, 0)


def body(
    n, count, volume, cotangent, near, far, bias,
    output, grad,
    v_pad, g_pad, far_all, far_turned,
    local_sem, w_send, w_recv, x_send, x_recv, s_send, s_recv, c_send, c_recv,
):
    s = lax.axis_index("space")
    c = lax.axis_index("chan")
    pairs = n // 2
    pair, side = c // 2, c % 2
    sibling = c + 1 - 2 * side
    planes, rows, block = volume.shape[0], volume.shape[1], volume.shape[2]
    has_low, has_high = s > 0, s < count - 1

    barrier = pltpu.get_barrier_semaphore()
    for j in range(1, n):
        pl.semaphore_signal(
            barrier, inc=1, device_id={"chan": lax.rem(c + j, n)}, device_id_type=MESH
        )

    @pl.when(has_low)
    def _():
        pl.semaphore_signal(barrier, inc=1, device_id={"space": s - 1}, device_id_type=MESH)

    @pl.when(has_high)
    def _():
        pl.semaphore_signal(barrier, inc=1, device_id={"space": s + 1}, device_id_type=MESH)

    peers = n - 1 + has_low.astype(jnp.int32) + has_high.astype(jnp.int32)
    pl.semaphore_wait(barrier, peers)

    def at(pad, first, size, owner):
        return pad.at[
            pl.ds(1, planes),
            pl.ds(first, size),
            pl.ds(pl.multiple_of(owner * block, block), block),
        ]

    spans = ((1, 1), (rows, 1), (2, rows - 2))
    sources = (volume, cotangent)
    pads = (v_pad, g_pad)

    def from_pair(j):
        return lax.rem(pair - j + pairs, pairs) * 2 + side

    def x_copy(t, j, i, arriving):
        first, size = spans[i]
        if arriving:
            src = dst = at(pads[t], first, size, from_pair(j))
        else:
            src = sources[t].at[:, pl.ds(first - 1, size)]
            dst = at(pads[t], first, size, c)
        return pltpu.make_async_remote_copy(
            src_ref=src, dst_ref=dst,
            send_sem=x_send.at[t, j - 1, i], recv_sem=x_recv.at[t, j - 1, i],
            device_id={"chan": lax.rem(pair + j, pairs) * 2 + side}, device_id_type=MESH,
        )

    def s_copy(t, j, way, arriving):
        landing = rows + 1 if way == 0 else 0
        owner = c if j == 0 else from_pair(j)
        dst = at(pads[t], landing, 1, owner)
        if arriving:
            src = dst
        elif j == 0:
            src = sources[t].at[:, pl.ds(0 if way == 0 else rows - 1, 1)]
        else:
            src = at(pads[t], 1 if way == 0 else rows, 1, owner)
        return pltpu.make_async_remote_copy(
            src_ref=src, dst_ref=dst,
            send_sem=s_send.at[t, j, way], recv_sem=s_recv.at[t, j, way],
            device_id={"space": s - 1 if way == 0 else s + 1}, device_id_type=MESH,
        )

    def c_copy(t, slot, arriving):
        reach = c if not arriving else sibling
        mine = reach % 2
        if slot == 0:
            dst = at(pads[t], 1, rows, reach)
            src = dst if arriving else sources[t]
        elif slot <= 3 * (pairs - 1):
            j, i = (slot - 1) // 3 + 1, (slot - 1) % 3
            owner = lax.rem(pair - j + pairs, pairs) * 2 + mine
            dst = src = at(pads[t], spans[i][0], spans[i][1], owner)
        else:
            rest = slot - 1 - 3 * (pairs - 1)
            j, way = rest // 2, rest % 2
            owner = lax.rem(pair - j + pairs, pairs) * 2 + mine
            dst = src = at(pads[t], rows + 1 if way == 0 else 0, 1, owner)
        return pltpu.make_async_remote_copy(
            src_ref=src, dst_ref=dst,
            send_sem=c_send.at[t, slot], recv_sem=c_recv.at[t, slot],
            device_id={"chan": sibling}, device_id_type=MESH,
        )

    def edge_slot(j, way):
        return 1 + 3 * (pairs - 1) + 2 * j + way

    def local(t):
        return pltpu.make_async_copy(sources[t], at(pads[t], 1, rows, c), local_sem.at[t])

    def w_copy(j, arriving):
        owner = lax.rem(c - j + n, n) if arriving else c
        target = lax.rem(c + j, n)
        dst = far_all.at[:, pl.ds(pl.multiple_of(owner * block, block), block)]
        return pltpu.make_async_remote_copy(
            src_ref=dst if arriving else far.at[target], dst_ref=dst,
            send_sem=w_send.at[j], recv_sem=w_recv.at[j],
            device_id={"chan": target}, device_id_type=MESH,
        )

    def sends_to(way):
        return has_low if way == 0 else has_high

    def gets_from(way):
        return has_high if way == 0 else has_low

    def when(flag, act):
        pl.when(flag)(act)

    def start_edges(t):
        for j in range(1, pairs):
            for i in (0, 1):
                x_copy(t, j, i, False).start()
        for way in (0, 1):
            when(sends_to(way), lambda way=way: s_copy(t, 0, way, False).start())

    def start_rest(t):
        for j in range(1, pairs):
            x_copy(t, j, 2, False).start()
        c_copy(t, 0, False).start()
        local(t).start()

    def pass_edges(t):
        for j in range(1, pairs):
            for way in (0, 1):
                x_copy(t, j, way, True).wait_recv()
                when(sends_to(way), lambda way=way, j=j: s_copy(t, j, way, False).start())
        for j in range(1, pairs):
            for way in (0, 1):
                c_copy(t, 1 + 3 * (j - 1) + way, False).start()

    def pass_halo(t, j):
        for way in (0, 1):

            def act(way=way):
                s_copy(t, j, way, True).wait_recv()
                c_copy(t, edge_slot(j, way), False).start()

            when(gets_from(way), act)

    def pass_middle(t):
        for j in range(1, pairs):
            x_copy(t, j, 2, True).wait_recv()
            c_copy(t, 3 * j, False).start()

    def collect(t):
        local(t).wait()
        for slot in range(1 + 3 * (pairs - 1)):
            c_copy(t, slot, True).wait_recv()
        for j in range(pairs):
            for way in (0, 1):
                when(
                    gets_from(way),
                    lambda way=way, j=j: c_copy(t, edge_slot(j, way), True).wait_recv(),
                )

    def finish(t):
        for j in range(1, pairs):
            for i in range(3):
                x_copy(t, j, i, False).wait_send()
        for slot in range(1 + 3 * (pairs - 1)):
            c_copy(t, slot, False).wait_send()
        for j in range(pairs):
            for way in (0, 1):
                when(sends_to(way), lambda way=way, j=j: s_copy(t, j, way, False).wait_send())
                when(
                    gets_from(way),
                    lambda way=way, j=j: c_copy(t, edge_slot(j, way), False).wait_send(),
                )

    start_edges(0)
    start_rest(0)
    own = pltpu.make_async_copy(
        far.at[c], far_all.at[:, pl.ds(pl.multiple_of(c * block, block), block)], local_sem.at[2]
    )
    own.start()
    for j in range(1, n):
        w_copy(j, False).start()

    for pad in pads:
        blank = jnp.zeros(pad.shape[1:], pad.dtype)
        pad[0] = blank
        pad[planes + 1] = blank

        @pl.when(jnp.logical_not(has_low))
        def _():
            pad[:, 0] = jnp.zeros((planes + 2,) + pad.shape[2:], pad.dtype)

        @pl.when(jnp.logical_not(has_high))
        def _():
            pad[:, rows + 1] = jnp.zeros((planes + 2,) + pad.shape[2:], pad.dtype)

    pass_edges(0)
    start_edges(1)
    pass_halo(0, 0)
    pass_middle(0)
    start_rest(1)
    for j in range(1, n):
        w_copy(j, True).wait_recv()
    own.wait()
    for k in range(9):
        depth = far_all.shape[1]
        far_turned[:, k * depth : (k + 1) * depth] = far_all[k].T[: 3 * block]
    for j in range(1, pairs):
        pass_halo(0, j)
    pass_edges(1)
    collect(0)
    half = planes // 2
    convolve(v_pad, near, bias, output, 0, half)
    pass_halo(1, 0)
    pass_middle(1)
    convolve(v_pad, near, bias, output, half, planes)
    for j in range(1, pairs):
        pass_halo(1, j)
    collect(1)
    convolve(g_pad, far_turned, None, grad, 0, planes)
    for j in range(1, n):
        w_copy(j, False).wait_send()
    finish(0)
    finish(1)


def per_device(n, count, volume, kernel, bias, cotangent):
    planes, rows, block, cells = volume.shape
    channels = kernel.shape[1]
    taps = kernel.reshape(3, 3, 3, channels, block)
    near = taps.transpose(2, 4, 0, 1, 3).reshape(3 * block, 9 * channels)
    far = taps[::-1, ::-1, ::-1].reshape(9, 3, n, block, block)
    far = far.transpose(2, 0, 4, 1, 3).reshape(n, 9, block, 3 * block)
    far = jnp.pad(far, ((0, 0), (0, 0), (0, 0), (0, channels - 3 * block)))
    wide_bias = jnp.broadcast_to(bias[:, None], (block, cells))
    pairs = n // 2
    slots = 1 + 3 * (pairs - 1) + 2 * pairs
    dma = pltpu.SemaphoreType.DMA
    padded = pltpu.VMEM((planes + 2, rows + 2, channels, cells), volume.dtype)
    whole = pl.BlockSpec(memory_space=pltpu.VMEM)
    shape = jax.ShapeDtypeStruct(volume.shape, volume.dtype)
    others = max(pairs - 1, 1)
    return pl.pallas_call(
        functools.partial(body, n, count),
        out_shape=(shape, shape),
        in_specs=[pl.BlockSpec(memory_space=pl.ANY)] * 2 + [whole] * 3,
        out_specs=(whole, whole),
        scratch_shapes=[
            padded,
            padded,
            pltpu.VMEM((9, channels, channels), kernel.dtype),
            pltpu.VMEM((3 * block, 9 * channels), kernel.dtype),
            dma((3,)),
            dma((n,)),
            dma((n,)),
            dma((2, others, 3)),
            dma((2, others, 3)),
            dma((2, pairs, 2)),
            dma((2, pairs, 2)),
            dma((2, slots)),
            dma((2, slots)),
        ],
        compiler_params=pltpu.CompilerParams(
            collective_id=0, has_side_effects=True, vmem_limit_bytes=48 * 1024 * 1024
        ),
        cost_estimate=pl.CostEstimate(
            flops=4 * 27 * planes * rows * cells * block * channels,
            bytes_accessed=4 * 2 * planes * rows * block * cells,
            transcendentals=0,
        ),
    )(volume, cotangent, near, far, wide_bias)


def solution(mesh):
    n, count = mesh.shape["chan"], mesh.shape["space"]
    spec = P(None, "space", "chan", None)
    return jax.shard_map(
        functools.partial(per_device, n, count),
        mesh=mesh,
        in_specs=(spec, P(None, None, "chan"), P("chan"), spec),
        out_specs=(spec, spec),
        check_vma=False,
    )
```

time: 112 us -> 49 us (0.44); the launches traced: 110 us -> 48.8 us
  Pallas kernels: 0 us -> 42.6 us
  matrix products: 35.7 us -> 0 us
  waiting for transfers between devices: 23 us -> 0 us
  between operations: 14.3 us -> 0.72 us
  local copies, waits for them, and re-layouts: 18.5 us -> 5.49 us
  starting transfers between devices: 9.76 us -> 0 us
  other arithmetic: 8.57 us -> 0 us
    pallas_call x0 -> x1, Pallas kernels: none -> 42.6 us  [per_device(): pl.pallas_call(functools.partial(body, n, count), out_shape=(shape, shape...]
    dot_general x30 -> x0, matrix products: 35.7 us -> none  [the longest x27 20.8 us: shifted_terms(): jnp.einsum('xyiz,io->xyoz', stacked, weight_now, preferred_element_type=j...]
    ppermute x4 -> x0, waiting for transfers between devices: 11 us -> none  [the longest x2 11 us: with_halo(): lax.ppermute(lax.slice_in_dim(block, block.shape[dim] - width, None, axis...]
    unnamed x28 -> x10, local copies, waits for them, and re-layouts: 13.1 us -> 2.31 us
    ppermute x4 -> x0, starting transfers between devices: 9.68 us -> none  [the longest x2 7.1 us: with_halo(): lax.ppermute(lax.slice_in_dim(block, block.shape[dim] - width, None, axis...]
    reduce_scatter x1 -> x0, waiting for transfers between devices: 8.9 us -> none  [per_device(): lax.psum_scatter(partials, 'chan', scatter_dimension=2, tiled=True)]
    concatenate x2 -> x0, other arithmetic: 6.27 us -> none  [with_halo(): block = jnp.concatenate([low, block, high], axis=dim)]
    slice x2 -> x0, local copies, waits for them, and re-layouts: 3.28 us -> none  [with_halo(): lax.slice_in_dim(block, block.shape[dim] - width, None, axis=dim)]
  transfers between devices with their start and end apart: 6 -> 0, of which waited for: 3 -> 0; matrix products, arithmetic and copies ran while one was open for 51% -> 0% of each run, Pallas kernels for 0% -> 0%
where the time goes in v1:
time: 49 us; the launch traced here: 48.8 us
  Pallas kernels  42.6 us (87%)
  local copies, waits for them, and re-layouts  5.49 us (11%)
  between operations  0.72 us (1%)
    pallas_call x1, Pallas kernels, per_device(): pl.pallas_call(functools.partial(body, n, count), out_shape=(shape, shape...  42.6 us
    unnamed x10, local copies, waits for them, and re-layouts  2.31 us

profile of v1, /device:TPU:1, one launch (start us, length us, event | category | flops | bytes accessed | tf_op | source)
XLA Modules:
  0.0 48.8 jit_solution(12031306160406291018)
XLA Ops:
  0.6 1.0 %rev.3 = bf16[3,3,3,128,32]{3,4,2,1,0:T(8,128)(2,1)S(1)} reverse(bf16[3,3,3,128,32]{3,4,2,1,0:T(8,128)(2,1)} %bitcast.9), dimensions={0,1,2} | reverse | bytes 442368 | tf_op jit(solution)/shard_map/rev | solution.py:288
  1.6 0.4 reshape.19
  1.9 0.8 %copy.8 = bf16[4,9,32,3,32]{4,3,2,1,0:T(4,128)(2,1)S(1)} copy(bf16[4,9,32,3,32]{4,0,2,3,1:T(4,128)(2,1)S(1)} %bitcast.8) | data formatting | bytes 442368 | tf_op jit(solution)/shard_map/transpose | solution.py:289
  2.8 0.0 copy-start.2
  2.8 0.6 %reshape.20 = bf16[4,9,32,96]{3,2,1,0:T(8,128)(2,1)S(1)} reshape(bf16[4,9,32,3,32]{4,3,2,1,0:T(4,128)(2,1)S(1)} %copy.8) | data formatting | bytes 442368 | tf_op jit(solution)/shard_map/reshape | solution.py:289
  3.4 0.0 copy-start.3
  3.4 0.0 copy-start
  3.4 0.0 copy-start.1
  3.4 0.1 pad.4.far
  3.5 0.3 copy-done.2
  3.7 0.2 copy.7
  3.9 0.2 reshape.18.near
  4.1 0.0 copy-done.3
  4.1 0.1 broadcast_in_dim.2.bias
  4.2 0.3 copy-done
  4.5 0.2 copy-done.1
  4.6 42.6 %shard_map.59 = (bf16[16,4,32,128]{3,2,1,0:T(8,128)(2,1)S(1)}, bf16[16,4,32,128]{3,2,1,0:T(8,128)(2,1)S(1)}) custom-call(bf16[16,4,32,128]{3,2,1,0:T(8,128)(2,1)S(1)} %copy-done, bf16[16,4,32,128]{3,2,1,0:T(8,128)(2,1)S(1)} %copy-done.1, bf16[96,1152]{1,0:T(8,128)(2,1)S(1)} %reshape.18.near, bf16[4,9,32,128]{3,2,1,0:T(8,128)(2,1)S(1)} %pad.4.far, ...), custom_call_target="tpu_custom_call" | custom-call | flops 3623878656 | bytes 2097152 | tf_op jit(solution)/shard_map/pallas_call | solution.py:299
  47.2 0.8 %copy.11 = bf16[16,4,32,128]{3,2,1,0:T(8,128)(2,1)} copy(bf16[16,4,32,128]{3,2,1,0:T(8,128)(2,1)S(1)} %get-tuple-element.4) | data formatting | bytes 1048576
  48.0 0.8 %copy.12 = bf16[16,4,32,128]{3,2,1,0:T(8,128)(2,1)} copy(bf16[16,4,32,128]{3,2,1,0:T(8,128)(2,1)S(1)} %get-tuple-element.5) | data formatting | bytes 1048576
Async XLA Ops:
  2.8 0.9 %copy-start.2 = (bf16[27,128,32]{1,2,0:T(8,128)(2,1)S(1)}, bf16[27,128,32]{1,2,0:T(8,128)(2,1)}, u32[]{:S(2)}) copy-start(bf16[27,128,32]{1,2,0:T(8,128)(2,1)} %param.5) | copy-start | bytes 663556
  3.4 0.7 %copy-start.3 = (f32[32]{0:T(128)S(1)}, f32[32]{0:T(128)}, u32[]{:S(2)}) copy-start(f32[32]{0:T(128)} %param.6) | copy-start | bytes 388
  3.4 1.1 %copy-start = (bf16[16,4,32,128]{3,2,1,0:T(8,128)(2,1)S(1)}, bf16[16,4,32,128]{3,2,1,0:T(8,128)(2,1)}, u32[]{:S(2)}) copy-start(bf16[16,4,32,128]{3,2,1,0:T(8,128)(2,1)} %volume.1) | copy-start | bytes 1572868
  3.4 1.2 %copy-start.1 = (bf16[16,4,32,128]{3,2,1,0:T(8,128)(2,1)S(1)}, bf16[16,4,32,128]{3,2,1,0:T(8,128)(2,1)}, u32[]{:S(2)}) copy-start(bf16[16,4,32,128]{3,2,1,0:T(8,128)(2,1)} %cotangent.1) | copy-start | bytes 1572868

commit v2 on v1

--- a/solution.py
+++ b/solution.py
@@ -48,9 +48,9 @@
 
 
 def body(
-    n, count, volume, cotangent, near, far, bias,
+    n, count, parts, volume, cotangent, turned_kernel, bias,
     output, grad,
-    v_pad, g_pad, far_all, far_turned,
+    v_pad, g_pad, near, far, far_all, far_turned,
     local_sem, w_send, w_recv, x_send, x_recv, s_send, s_recv, c_send, c_recv,
 ):
     s = lax.axis_index("space")
@@ -59,6 +59,7 @@
     pair, side = c // 2, c % 2
     sibling = c + 1 - 2 * side
     planes, rows, block = volume.shape[0], volume.shape[1], volume.shape[2]
+    channels = turned_kernel.shape[2]
     has_low, has_high = s > 0, s < count - 1
 
     barrier = pltpu.get_barrier_semaphore()
@@ -78,16 +79,20 @@
     peers = n - 1 + has_low.astype(jnp.int32) + has_high.astype(jnp.int32)
     pl.semaphore_wait(barrier, peers)
 
-    def at(pad, first, size, owner):
-        return pad.at[
-            pl.ds(1, planes),
+    sources = [(volume, cotangent)[part[0]] for part in parts]
+    pads = [(v_pad, g_pad)[part[0]] for part in parts]
+
+    def at(t, first, size, owner):
+        return pads[t].at[
+            pl.ds(1 + parts[t][1], parts[t][2]),
             pl.ds(first, size),
             pl.ds(pl.multiple_of(owner * block, block), block),
         ]
 
+    def source(t, first, size):
+        return sources[t].at[pl.ds(parts[t][1], parts[t][2]), pl.ds(first, size)]
+
     spans = ((1, 1), (rows, 1), (2, rows - 2))
-    sources = (volume, cotangent)
-    pads = (v_pad, g_pad)
 
     def from_pair(j):
         return lax.rem(pair - j + pairs, pairs) * 2 + side
@@ -95,10 +100,10 @@
     def x_copy(t, j, i, arriving):
         first, size = spans[i]
         if arriving:
-            src = dst = at(pads[t], first, size, from_pair(j))
+            src = dst = at(t, first, size, from_pair(j))
         else:
-            src = sources[t].at[:, pl.ds(first - 1, size)]
-            dst = at(pads[t], first, size, c)
+            src = source(t, first - 1, size)
+            dst = at(t, first, size, c)
         return pltpu.make_async_remote_copy(
             src_ref=src, dst_ref=dst,
             send_sem=x_send.at[t, j - 1, i], recv_sem=x_recv.at[t, j - 1, i],
@@ -108,13 +113,13 @@
     def s_copy(t, j, way, arriving):
         landing = rows + 1 if way == 0 else 0
         owner = c if j == 0 else from_pair(j)
-        dst = at(pads[t], landing, 1, owner)
+        dst = at(t, landing, 1, owner)
         if arriving:
             src = dst
         elif j == 0:
-            src = sources[t].at[:, pl.ds(0 if way == 0 else rows - 1, 1)]
+            src = source(t, 0 if way == 0 else rows - 1, 1)
         else:
-            src = at(pads[t], 1 if way == 0 else rows, 1, owner)
+            src = at(t, 1 if way == 0 else rows, 1, owner)
         return pltpu.make_async_remote_copy(
             src_ref=src, dst_ref=dst,
             send_sem=s_send.at[t, j, way], recv_sem=s_recv.at[t, j, way],
@@ -125,17 +130,17 @@
         reach = c if not arriving else sibling
         mine = reach % 2
         if slot == 0:
-            dst = at(pads[t], 1, rows, reach)
-            src = dst if arriving else sources[t]
+            dst = at(t, 1, rows, reach)
+            src = dst if arriving else source(t, 0, rows)
         elif slot <= 3 * (pairs - 1):
             j, i = (slot - 1) // 3 + 1, (slot - 1) % 3
             owner = lax.rem(pair - j + pairs, pairs) * 2 + mine
-            dst = src = at(pads[t], spans[i][0], spans[i][1], owner)
+            dst = src = at(t, spans[i][0], spans[i][1], owner)
         else:
             rest = slot - 1 - 3 * (pairs - 1)
             j, way = rest // 2, rest % 2
             owner = lax.rem(pair - j + pairs, pairs) * 2 + mine
-            dst = src = at(pads[t], rows + 1 if way == 0 else 0, 1, owner)
+            dst = src = at(t, rows + 1 if way == 0 else 0, 1, owner)
         return pltpu.make_async_remote_copy(
             src_ref=src, dst_ref=dst,
             send_sem=c_send.at[t, slot], recv_sem=c_recv.at[t, slot],
@@ -146,7 +151,7 @@
         return 1 + 3 * (pairs - 1) + 2 * j + way
 
     def local(t):
-        return pltpu.make_async_copy(sources[t], at(pads[t], 1, rows, c), local_sem.at[t])
+        return pltpu.make_async_copy(source(t, 0, rows), at(t, 1, rows, c), local_sem.at[t])
 
     def w_copy(j, arriving):
         owner = lax.rem(c - j + n, n) if arriving else c
@@ -228,16 +233,36 @@
                     lambda way=way, j=j: c_copy(t, edge_slot(j, way), False).wait_send(),
                 )
 
-    start_edges(0)
-    start_rest(0)
+    for t in (0, 1):
+        start_edges(t)
+        start_rest(t)
+
+    lane = lax.broadcasted_iota(jnp.int32, (block, channels), 1)
+    for ab in range(9):
+        packed = [jnp.zeros((block, channels), jnp.float32) for _ in range(n)]
+        for q in range(3):
+            turned = turned_kernel[26 - (3 * ab + q)].astype(jnp.float32)
+            near_row, near_column = (2 - q) * block, (8 - ab) * channels
+            near[near_row : near_row + block, near_column : near_column + channels] = (
+                turned.astype(near.dtype)
+            )
+            inside = (lane >= q * block) & (lane < (q + 1) * block)
+            for target in range(n):
+                shift = (q - target) * block % channels
+                moved = turned if shift == 0 else pltpu.roll(turned, shift, 1)
+                packed[target] = jnp.where(inside, moved, packed[target])
+        for target in range(n):
+            far[target, ab] = packed[target].astype(far.dtype)
     own = pltpu.make_async_copy(
-        far.at[c], far_all.at[:, pl.ds(pl.multiple_of(c * block, block), block)], local_sem.at[2]
+        far.at[c],
+        far_all.at[:, pl.ds(pl.multiple_of(c * block, block), block)],
+        local_sem.at[len(parts)],
     )
     own.start()
     for j in range(1, n):
         w_copy(j, False).start()
 
-    for pad in pads:
+    for pad in (v_pad, g_pad):
         blank = jnp.zeros(pad.shape[1:], pad.dtype)
         pad[0] = blank
         pad[planes + 1] = blank
@@ -250,45 +275,60 @@
         def _():
             pad[:, rows + 1] = jnp.zeros((planes + 2,) + pad.shape[2:], pad.dtype)
 
+    def pass_far(t):
+        for j in range(1, pairs):
+            pass_halo(t, j)
+
+    split = parts[0][2] - 1
+    middle = (split + planes) // 2
+    g_split = parts[2][2] - 1
     pass_edges(0)
-    start_edges(1)
     pass_halo(0, 0)
     pass_middle(0)
-    start_rest(1)
+    start_edges(2)
+    start_rest(2)
+    pass_edges(1)
+    pass_halo(1, 0)
+    pass_far(0)
+    pass_middle(1)
+    start_edges(3)
+    start_rest(3)
+    collect(0)
+    convolve(v_pad, near, bias, output, 0, split)
+    pass_edges(2)
+    pass_halo(2, 0)
+    pass_far(1)
+    collect(1)
+    convolve(v_pad, near, bias, output, split, middle)
+    pass_middle(2)
+    pass_edges(3)
+    pass_halo(3, 0)
+    convolve(v_pad, near, bias, output, middle, planes)
+    pass_middle(3)
+    pass_far(2)
     for j in range(1, n):
         w_copy(j, True).wait_recv()
     own.wait()
     for k in range(9):
         depth = far_all.shape[1]
         far_turned[:, k * depth : (k + 1) * depth] = far_all[k].T[: 3 * block]
-    for j in range(1, pairs):
-        pass_halo(0, j)
-    pass_edges(1)
-    collect(0)
-    half = planes // 2
-    convolve(v_pad, near, bias, output, 0, half)
-    pass_halo(1, 0)
-    pass_middle(1)
-    convolve(v_pad, near, bias, output, half, planes)
-    for j in range(1, pairs):
-        pass_halo(1, j)
-    collect(1)
-    convolve(g_pad, far_turned, None, grad, 0, planes)
+    collect(2)
+    pass_far(3)
+    convolve(g_pad, far_turned, None, grad, 0, g_split)
+    collect(3)
+    convolve(g_pad, far_turned, None, grad, g_split, planes)
     for j in range(1, n):
         w_copy(j, False).wait_send()
-    finish(0)
-    finish(1)
+    for t in range(len(parts)):
+        finish(t)
 
 
 def per_device(n, count, volume, kernel, bias, cotangent):
     planes, rows, block, cells = volume.shape
     channels = kernel.shape[1]
-    taps = kernel.reshape(3, 3, 3, channels, block)
-    near = taps.transpose(2, 4, 0, 1, 3).reshape(3 * block, 9 * channels)
-    far = taps[::-1, ::-1, ::-1].reshape(9, 3, n, block, block)
-    far = far.transpose(2, 0, 4, 1, 3).reshape(n, 9, block, 3 * block)
-    far = jnp.pad(far, ((0, 0), (0, 0), (0, 0), (0, channels - 3 * block)))
     wide_bias = jnp.broadcast_to(bias[:, None], (block, cells))
+    half = planes // 2
+    parts = [(t, first, size) for t in (0, 1) for first, size in ((0, half), (half, planes - half))]
     pairs = n // 2
     slots = 1 + 3 * (pairs - 1) + 2 * pairs
     dma = pltpu.SemaphoreType.DMA
@@ -297,24 +337,26 @@
     shape = jax.ShapeDtypeStruct(volume.shape, volume.dtype)
     others = max(pairs - 1, 1)
     return pl.pallas_call(
-        functools.partial(body, n, count),
+        functools.partial(body, n, count, parts),
         out_shape=(shape, shape),
-        in_specs=[pl.BlockSpec(memory_space=pl.ANY)] * 2 + [whole] * 3,
+        in_specs=[pl.BlockSpec(memory_space=pl.ANY)] * 2 + [whole] * 2,
         out_specs=(whole, whole),
         scratch_shapes=[
             padded,
             padded,
+            pltpu.VMEM((3 * block, 9 * channels), kernel.dtype),
+            pltpu.VMEM((n, 9, block, channels), kernel.dtype),
             pltpu.VMEM((9, channels, channels), kernel.dtype),
             pltpu.VMEM((3 * block, 9 * channels), kernel.dtype),
-            dma((3,)),
+            dma((5,)),
             dma((n,)),
             dma((n,)),
-            dma((2, others, 3)),
-            dma((2, others, 3)),
-            dma((2, pairs, 2)),
-            dma((2, pairs, 2)),
-            dma((2, slots)),
-            dma((2, slots)),
+            dma((4, others, 3)),
+            dma((4, others, 3)),
+            dma((4, pairs, 2)),
+            dma((4, pairs, 2)),
+            dma((4, slots)),
+            dma((4, slots)),
         ],
         compiler_params=pltpu.CompilerParams(
             collective_id=0, has_side_effects=True, vmem_limit_bytes=48 * 1024 * 1024
@@ -324,7 +366,7 @@
             bytes_accessed=4 * 2 * planes * rows * block * cells,
             transcendentals=0,
         ),
-    )(volume, cotangent, near, far, wide_bias)
+    )(volume, cotangent, kernel.transpose(0, 2, 1), wide_bias)
 
 
 def solution(mesh):

time: 49 us -> 46.5 us (0.949)
  Pallas kernels: 42.6 us -> 40.3 us
    unnamed x10, local copies, waits for them, and re-layouts: 2.31 us -> 5.26 us
    pallas_call x1, Pallas kernels: 42.6 us -> 40.3 us  [per_device(): pl.pallas_call(functools.partial(body, n, count, parts), out_shape=(shape...]
    reshape x3 -> x0, local copies, waits for them, and re-layouts: 1.1 us -> none  [the longest x1 0.55 us: per_device(): far = far.transpose(2, 0, 4, 1, 3).reshape(n, 9, block, 3 * block)]
    transpose x2 -> x0, local copies, waits for them, and re-layouts: 0.99 us -> none  [the longest x1 0.84 us: per_device(): far = far.transpose(2, 0, 4, 1, 3).reshape(n, 9, block, 3 * block)]
    rev x1 -> x0, local copies, waits for them, and re-layouts: 0.95 us -> none  [per_device(): far = taps[::-1, ::-1, ::-1].reshape(9, 3, n, block, block)]
where the time goes in v2:
time: 46.5 us; the launch traced here: 46.3 us
  Pallas kernels  40.3 us (87%)
  local copies, waits for them, and re-layouts  5.33 us (11%)
  between operations  0.65 us (1%)
    pallas_call x1, Pallas kernels, per_device(): pl.pallas_call(functools.partial(body, n, count, parts), out_shape=(shape...  40.3 us
    unnamed x10, local copies, waits for them, and re-layouts  5.26 us

profile of v2, /device:TPU:1, one launch (start us, length us, event | category | flops | bytes accessed | tf_op | source)
XLA Modules:
  0.0 46.3 jit_solution(2626026814551172088)
XLA Ops:
  0.6 0.0 copy-start.3
  0.6 0.6 %copy-done.3 = f32[32]{0:T(128)S(1)} copy-done((f32[32]{0:T(128)S(1)}, f32[32]{0:T(128)}, u32[]{:S(2)}) %copy-start.3) | copy-done | bytes 152
  1.3 0.1 broadcast_in_dim.2.bias
  1.4 0.0 copy-start
  1.4 1.0 %copy-done = bf16[16,4,32,128]{3,2,1,0:T(8,128)(2,1)S(1)} copy-done((bf16[16,4,32,128]{3,2,1,0:T(8,128)(2,1)S(1)}, bf16[16,4,32,128]{3,2,1,0:T(8,128)(2,1)}, u32[]{:S(2)}) %copy-start) | copy-done | bytes 524312
  2.4 0.0 copy-start.1
  2.4 1.0 %copy-done.1 = bf16[16,4,32,128]{3,2,1,0:T(8,128)(2,1)S(1)} copy-done((bf16[16,4,32,128]{3,2,1,0:T(8,128)(2,1)S(1)}, bf16[16,4,32,128]{3,2,1,0:T(8,128)(2,1)}, u32[]{:S(2)}) %copy-start.1) | copy-done | bytes 524312
  3.4 0.0 copy-start.2
  3.4 0.9 %copy-done.2 = bf16[27,128,32]{1,2,0:T(8,128)(2,1)S(1)} copy-done((bf16[27,128,32]{1,2,0:T(8,128)(2,1)S(1)}, bf16[27,128,32]{1,2,0:T(8,128)(2,1)}, u32[]{:S(2)}) %copy-start.2) | copy-done | bytes 221208
  4.4 40.3 %shard_map.59 = (bf16[16,4,32,128]{3,2,1,0:T(8,128)(2,1)S(1)}, bf16[16,4,32,128]{3,2,1,0:T(8,128)(2,1)S(1)}) custom-call(bf16[16,4,32,128]{3,2,1,0:T(8,128)(2,1)S(1)} %copy-done, bf16[16,4,32,128]{3,2,1,0:T(8,128)(2,1)S(1)} %copy-done.1, bf16[27,32,128]{2,1,0:T(8,128)(2,1)S(1)} %bitcast.1, f32[32,128]{1,0:T(8,128)S(1)} %broadcast_in_dim.2.bias), custom_call_target="tpu_custom_call" | custom-call | flops 3623878656 | bytes 2097152 | tf_op jit(solution)/shard_map/pallas_call | solution.py:339
  44.7 0.8 %copy.8 = bf16[16,4,32,128]{3,2,1,0:T(8,128)(2,1)} copy(bf16[16,4,32,128]{3,2,1,0:T(8,128)(2,1)S(1)} %get-tuple-element.4) | data formatting | bytes 1048576
  45.5 0.8 %copy.9 = bf16[16,4,32,128]{3,2,1,0:T(8,128)(2,1)} copy(bf16[16,4,32,128]{3,2,1,0:T(8,128)(2,1)S(1)} %get-tuple-element.5) | data formatting | bytes 1048576
Async XLA Ops:
  0.6 0.7 %copy-start.3 = (f32[32]{0:T(128)S(1)}, f32[32]{0:T(128)}, u32[]{:S(2)}) copy-start(f32[32]{0:T(128)} %param.6) | copy-start | bytes 388
  1.4 1.0 %copy-start = (bf16[16,4,32,128]{3,2,1,0:T(8,128)(2,1)S(1)}, bf16[16,4,32,128]{3,2,1,0:T(8,128)(2,1)}, u32[]{:S(2)}) copy-start(bf16[16,4,32,128]{3,2,1,0:T(8,128)(2,1)} %volume.1) | copy-start | bytes 1572868
  2.4 1.0 %copy-start.1 = (bf16[16,4,32,128]{3,2,1,0:T(8,128)(2,1)S(1)}, bf16[16,4,32,128]{3,2,1,0:T(8,128)(2,1)}, u32[]{:S(2)}) copy-start(bf16[16,4,32,128]{3,2,1,0:T(8,128)(2,1)} %cotangent.1) | copy-start | bytes 1572868
  3.4 0.9 %copy-start.2 = (bf16[27,128,32]{1,2,0:T(8,128)(2,1)S(1)}, bf16[27,128,32]{1,2,0:T(8,128)(2,1)}, u32[]{:S(2)}) copy-start(bf16[27,128,32]{1,2,0:T(8,128)(2,1)} %param.5) | copy-start | bytes 663556

commit v3 on v2

--- a/solution.py
+++ b/solution.py
@@ -48,9 +48,9 @@
 
 
 def body(
-    n, count, parts, volume, cotangent, turned_kernel, bias,
+    n, count, parts, volume, cotangent, kernel_in, bias,
     output, grad,
-    v_pad, g_pad, near, far, far_all, far_turned,
+    turned_kernel, v_pad, g_pad, near, far, far_all, far_turned,
     local_sem, w_send, w_recv, x_send, x_recv, s_send, s_recv, c_send, c_recv,
 ):
     s = lax.axis_index("space")
@@ -60,24 +60,9 @@
     sibling = c + 1 - 2 * side
     planes, rows, block = volume.shape[0], volume.shape[1], volume.shape[2]
     channels = turned_kernel.shape[2]
+    fetch = pltpu.make_async_copy(kernel_in, turned_kernel, local_sem.at[len(parts) + 1])
+    fetch.start()
     has_low, has_high = s > 0, s < count - 1
-
-    barrier = pltpu.get_barrier_semaphore()
-    for j in range(1, n):
-        pl.semaphore_signal(
-            barrier, inc=1, device_id={"chan": lax.rem(c + j, n)}, device_id_type=MESH
-        )
-
-    @pl.when(has_low)
-    def _():
-        pl.semaphore_signal(barrier, inc=1, device_id={"space": s - 1}, device_id_type=MESH)
-
-    @pl.when(has_high)
-    def _():
-        pl.semaphore_signal(barrier, inc=1, device_id={"space": s + 1}, device_id_type=MESH)
-
-    peers = n - 1 + has_low.astype(jnp.int32) + has_high.astype(jnp.int32)
-    pl.semaphore_wait(barrier, peers)
 
     sources = [(volume, cotangent)[part[0]] for part in parts]
     pads = [(v_pad, g_pad)[part[0]] for part in parts]
@@ -102,8 +87,7 @@
         if arriving:
             src = dst = at(t, first, size, from_pair(j))
         else:
-            src = source(t, first - 1, size)
-            dst = at(t, first, size, c)
+            src = dst = at(t, first, size, c)
         return pltpu.make_async_remote_copy(
             src_ref=src, dst_ref=dst,
             send_sem=x_send.at[t, j - 1, i], recv_sem=x_recv.at[t, j - 1, i],
@@ -116,8 +100,6 @@
         dst = at(t, landing, 1, owner)
         if arriving:
             src = dst
-        elif j == 0:
-            src = source(t, 0 if way == 0 else rows - 1, 1)
         else:
             src = at(t, 1 if way == 0 else rows, 1, owner)
         return pltpu.make_async_remote_copy(
@@ -130,8 +112,7 @@
         reach = c if not arriving else sibling
         mine = reach % 2
         if slot == 0:
-            dst = at(t, 1, rows, reach)
-            src = dst if arriving else source(t, 0, rows)
+            dst = src = at(t, 1, rows, reach)
         elif slot <= 3 * (pairs - 1):
             j, i = (slot - 1) // 3 + 1, (slot - 1) % 3
             owner = lax.rem(pair - j + pairs, pairs) * 2 + mine
@@ -183,7 +164,6 @@
         for j in range(1, pairs):
             x_copy(t, j, 2, False).start()
         c_copy(t, 0, False).start()
-        local(t).start()
 
     def pass_edges(t):
         for j in range(1, pairs):
@@ -209,7 +189,6 @@
             c_copy(t, 3 * j, False).start()
 
     def collect(t):
-        local(t).wait()
         for slot in range(1 + 3 * (pairs - 1)):
             c_copy(t, slot, True).wait_recv()
         for j in range(pairs):
@@ -233,11 +212,33 @@
                     lambda way=way, j=j: c_copy(t, edge_slot(j, way), False).wait_send(),
                 )
 
-    for t in (0, 1):
+    for t in range(4):
+        local(t).start()
+
+    barrier = pltpu.get_barrier_semaphore()
+    for j in range(1, n):
+        pl.semaphore_signal(
+            barrier, inc=1, device_id={"chan": lax.rem(c + j, n)}, device_id_type=MESH
+        )
+
+    @pl.when(has_low)
+    def _():
+        pl.semaphore_signal(barrier, inc=1, device_id={"space": s - 1}, device_id_type=MESH)
+
+    @pl.when(has_high)
+    def _():
+        pl.semaphore_signal(barrier, inc=1, device_id={"space": s + 1}, device_id_type=MESH)
+
+    peers = n - 1 + has_low.astype(jnp.int32) + has_high.astype(jnp.int32)
+    pl.semaphore_wait(barrier, peers)
+
+    for t in range(4):
+        local(t).wait()
         start_edges(t)
         start_rest(t)
 
     lane = lax.broadcasted_iota(jnp.int32, (block, channels), 1)
+    fetch.wait()
     for ab in range(9):
         packed = [jnp.zeros((block, channels), jnp.float32) for _ in range(n)]
         for q in range(3):
@@ -285,14 +286,10 @@
     pass_edges(0)
     pass_halo(0, 0)
     pass_middle(0)
-    start_edges(2)
-    start_rest(2)
     pass_edges(1)
     pass_halo(1, 0)
     pass_far(0)
     pass_middle(1)
-    start_edges(3)
-    start_rest(3)
     collect(0)
     convolve(v_pad, near, bias, output, 0, split)
     pass_edges(2)
@@ -339,16 +336,17 @@
     return pl.pallas_call(
         functools.partial(body, n, count, parts),
         out_shape=(shape, shape),
-        in_specs=[pl.BlockSpec(memory_space=pl.ANY)] * 2 + [whole] * 2,
+        in_specs=[pl.BlockSpec(memory_space=pl.ANY)] * 3 + [whole],
         out_specs=(whole, whole),
         scratch_shapes=[
+            pltpu.VMEM((27, block, channels), kernel.dtype),
             padded,
             padded,
             pltpu.VMEM((3 * block, 9 * channels), kernel.dtype),
             pltpu.VMEM((n, 9, block, channels), kernel.dtype),
             pltpu.VMEM((9, channels, channels), kernel.dtype),
             pltpu.VMEM((3 * block, 9 * channels), kernel.dtype),
-            dma((5,)),
+            dma((6,)),
             dma((n,)),
             dma((n,)),
             dma((4, others, 3)),
@@ -359,7 +357,7 @@
             dma((4, slots)),
         ],
         compiler_params=pltpu.CompilerParams(
-            collective_id=0, has_side_effects=True, vmem_limit_bytes=48 * 1024 * 1024
+            collective_id=0, has_side_effects=True, vmem_limit_bytes=62 * 1024 * 1024
         ),
         cost_estimate=pl.CostEstimate(
             flops=4 * 27 * planes * rows * cells * block * channels,

time: 46.5 us -> 46.3 us (level)
  the two profiles are of different devices: /device:TPU:1 before, /device:TPU:0 now
where the time goes in v3:
time: 46.3 us; the launch traced here: 46 us
  Pallas kernels  41.3 us (89%)
  local copies, waits for them, and re-layouts  4.06 us (9%)
  between operations  0.66 us (1%)
    pallas_call x1, Pallas kernels, per_device(): pl.pallas_call(functools.partial(body, n, count, parts), out_shape=(shape...  41.3 us
    unnamed x6, local copies, waits for them, and re-layouts  3.38 us

profile of v3, /device:TPU:0, one launch (start us, length us, event | category | flops | bytes accessed | tf_op | source)
XLA Modules:
  0.0 46.0 jit_solution(3096183450839134200)
XLA Ops:
  0.6 0.0 copy-start.1
  0.6 0.6 %copy-done.1 = f32[32]{0:T(128)S(1)} copy-done((f32[32]{0:T(128)S(1)}, f32[32]{0:T(128)}, u32[]{:S(2)}) %copy-start.1) | copy-done | bytes 152
  1.3 0.7 %broadcast_in_dim.2.bias = f32[32,128]{1,0:T(8,128)} broadcast(f32[32]{0:T(128)S(1)} %copy-done.1), dimensions={0} | broadcast | bytes 16512 | tf_op jit(solution)/shard_map/broadcast_in_dim | solution.py:326
  2.0 41.3 %shard_map.59 = (bf16[16,4,32,128]{3,2,1,0:T(8,128)(2,1)}, bf16[16,4,32,128]{3,2,1,0:T(8,128)(2,1)}) custom-call(bf16[16,4,32,128]{3,2,1,0:T(8,128)(2,1)} %volume.1, bf16[16,4,32,128]{3,2,1,0:T(8,128)(2,1)} %cotangent.1, bf16[27,32,128]{2,1,0:T(8,128)(2,1)} %bitcast.1, f32[32,128]{1,0:T(8,128)} %broadcast_in_dim.2.bias), custom_call_target="tpu_custom_call" | custom-call | flops 3623878656 | bytes 2097152 | tf_op jit(solution)/shard_map/pallas_call | solution.py:336
  43.3 0.0 copy-start
  43.3 1.9 %copy.8 = bf16[16,4,32,128]{3,2,1,0:T(8,128)(2,1)} copy(bf16[16,4,32,128]{3,2,1,0:T(8,128)(2,1)} %get-tuple-element.4) | data formatting | bytes 1048576
  45.2 0.0 copy-done
  45.2 0.8 %copy.9 = bf16[16,4,32,128]{3,2,1,0:T(8,128)(2,1)} copy(bf16[16,4,32,128]{3,2,1,0:T(8,128)(2,1)S(1)} %copy-done) | data formatting | bytes 1048576
Async XLA Ops:
  0.6 0.7 %copy-start.1 = (f32[32]{0:T(128)S(1)}, f32[32]{0:T(128)}, u32[]{:S(2)}) copy-start(f32[32]{0:T(128)} %param.6) | copy-start | bytes 388
  43.3 2.0 %copy-start = (bf16[16,4,32,128]{3,2,1,0:T(8,128)(2,1)S(1)}, bf16[16,4,32,128]{3,2,1,0:T(8,128)(2,1)}, u32[]{:S(2)}) copy-start(bf16[16,4,32,128]{3,2,1,0:T(8,128)(2,1)} %get-tuple-element.5) | copy-start | bytes 1572868

commit v4 on v3

--- a/solution.py
+++ b/solution.py
@@ -48,9 +48,9 @@
 
 
 def body(
-    n, count, parts, volume, cotangent, kernel_in, bias,
+    n, count, parts, volume, cotangent, kernel_in, bias_row,
     output, grad,
-    turned_kernel, v_pad, g_pad, near, far, far_all, far_turned,
+    turned_kernel, bias, v_pad, g_pad, near, far, far_all, far_turned,
     local_sem, w_send, w_recv, x_send, x_recv, s_send, s_recv, c_send, c_recv,
 ):
     s = lax.axis_index("space")
@@ -236,6 +236,13 @@
         local(t).wait()
         start_edges(t)
         start_rest(t)
+
+    square = (block, block)
+    diagonal = lax.broadcasted_iota(jnp.int32, square, 0) == lax.broadcasted_iota(
+        jnp.int32, square, 1
+    )
+    spread = jnp.where(diagonal, jnp.broadcast_to(bias_row[...], square), 0.0)
+    bias[...] = jnp.broadcast_to(jnp.sum(spread, axis=1, keepdims=True), bias.shape)
 
     lane = lax.broadcasted_iota(jnp.int32, (block, channels), 1)
     fetch.wait()
@@ -323,7 +330,6 @@
 def per_device(n, count, volume, kernel, bias, cotangent):
     planes, rows, block, cells = volume.shape
     channels = kernel.shape[1]
-    wide_bias = jnp.broadcast_to(bias[:, None], (block, cells))
     half = planes // 2
     parts = [(t, first, size) for t in (0, 1) for first, size in ((0, half), (half, planes - half))]
     pairs = n // 2
@@ -340,6 +346,7 @@
         out_specs=(whole, whole),
         scratch_shapes=[
             pltpu.VMEM((27, block, channels), kernel.dtype),
+            pltpu.VMEM((block, cells), jnp.float32),
             padded,
             padded,
             pltpu.VMEM((3 * block, 9 * channels), kernel.dtype),
@@ -364,7 +371,7 @@
             bytes_accessed=4 * 2 * planes * rows * block * cells,
             transcendentals=0,
         ),
-    )(volume, cotangent, kernel.transpose(0, 2, 1), wide_bias)
+    )(volume, cotangent, kernel.transpose(0, 2, 1), bias.reshape(1, block))
 
 
 def solution(mesh):

time: 46.3 us -> 44.8 us (0.968)
  local copies, waits for them, and re-layouts: 4.06 us -> 2.74 us
    broadcast_in_dim x1 -> x0, local copies, waits for them, and re-layouts: 0.67 us -> none  [per_device(): wide_bias = jnp.broadcast_to(bias[:, None], (block, cells))]
    unnamed x6 -> x4, local copies, waits for them, and re-layouts: 3.38 us -> 2.74 us
where the time goes in v4:
time: 44.8 us; the launch traced here: 44.7 us
  Pallas kernels  41.3 us (92%)
  local copies, waits for them, and re-layouts  2.74 us (6%)
  between operations  0.65 us (1%)
    pallas_call x1, Pallas kernels, per_device(): pl.pallas_call(functools.partial(body, n, count, parts), out_shape=(shape...  41.3 us
    unnamed x4, local copies, waits for them, and re-layouts  2.74 us

profile of v4, /device:TPU:0, one launch (start us, length us, event | category | flops | bytes accessed | tf_op | source)
XLA Modules:
  0.0 44.7 jit_solution(9554096660980564120)
XLA Ops:
  0.6 41.3 %shard_map.59 = (bf16[16,4,32,128]{3,2,1,0:T(8,128)(2,1)}, bf16[16,4,32,128]{3,2,1,0:T(8,128)(2,1)}) custom-call(bf16[16,4,32,128]{3,2,1,0:T(8,128)(2,1)} %volume.1, bf16[16,4,32,128]{3,2,1,0:T(8,128)(2,1)} %cotangent.1, bf16[27,32,128]{2,1,0:T(8,128)(2,1)} %bitcast.2, f32[1,32]{1,0:T(1,128)} %bitcast.3), custom_call_target="tpu_custom_call" | custom-call | flops 3623878656 | bytes 2097152 | tf_op jit(solution)/shard_map/pallas_call | solution.py:342
  41.9 0.0 copy-start
  41.9 1.9 %copy.8 = bf16[16,4,32,128]{3,2,1,0:T(8,128)(2,1)} copy(bf16[16,4,32,128]{3,2,1,0:T(8,128)(2,1)} %get-tuple-element.4) | data formatting | bytes 1048576
  43.9 0.0 copy-done
  43.9 0.8 %copy.9 = bf16[16,4,32,128]{3,2,1,0:T(8,128)(2,1)} copy(bf16[16,4,32,128]{3,2,1,0:T(8,128)(2,1)S(1)} %copy-done) | data formatting | bytes 1048576
Async XLA Ops:
  41.9 2.0 %copy-start = (bf16[16,4,32,128]{3,2,1,0:T(8,128)(2,1)S(1)}, bf16[16,4,32,128]{3,2,1,0:T(8,128)(2,1)}, u32[]{:S(2)}) copy-start(bf16[16,4,32,128]{3,2,1,0:T(8,128)(2,1)} %get-tuple-element.5) | copy-start | bytes 1572868

commit v5 on v4

--- a/solution.py
+++ b/solution.py
@@ -308,7 +308,6 @@
     pass_edges(3)
     pass_halo(3, 0)
     convolve(v_pad, near, bias, output, middle, planes)
-    pass_middle(3)
     pass_far(2)
     for j in range(1, n):
         w_copy(j, True).wait_recv()
@@ -317,8 +316,11 @@
         depth = far_all.shape[1]
         far_turned[:, k * depth : (k + 1) * depth] = far_all[k].T[: 3 * block]
     collect(2)
+    g_middle = g_split // 2
+    convolve(g_pad, far_turned, None, grad, 0, g_middle)
+    pass_middle(3)
     pass_far(3)
-    convolve(g_pad, far_turned, None, grad, 0, g_split)
+    convolve(g_pad, far_turned, None, grad, g_middle, g_split)
     collect(3)
     convolve(g_pad, far_turned, None, grad, g_split, planes)
     for j in range(1, n):
@@ -331,7 +333,9 @@
     planes, rows, block, cells = volume.shape
     channels = kernel.shape[1]
     half = planes // 2
-    parts = [(t, first, size) for t in (0, 1) for first, size in ((0, half), (half, planes - half))]
+    late = planes - planes * 3 // 8
+    cuts = (half, late)
+    parts = [(t, *span) for t in (0, 1) for span in ((0, cuts[t]), (cuts[t], planes - cuts[t]))]
     pairs = n // 2
     slots = 1 + 3 * (pairs - 1) + 2 * pairs
     dma = pltpu.SemaphoreType.DMA

time: 44.8 us -> 44 us (0.982)
  the two profiles are of different devices: /device:TPU:0 before, /device:TPU:1 now
where the time goes in v5:
time: 44 us; the launch traced here: 43.3 us
  Pallas kernels  39.9 us (91%)
  local copies, waits for them, and re-layouts  2.74 us (6%)
  between operations  0.65 us (1%)
    pallas_call x1, Pallas kernels, per_device(): pl.pallas_call(functools.partial(body, n, count, parts), out_shape=(shape...  39.9 us
    unnamed x4, local copies, waits for them, and re-layouts  2.74 us

profile of v5, /device:TPU:1, one launch (start us, length us, event | category | flops | bytes accessed | tf_op | source)
XLA Modules:
  0.0 43.3 jit_solution(8091695615876365817)
XLA Ops:
  0.6 39.9 %shard_map.59 = (bf16[16,4,32,128]{3,2,1,0:T(8,128)(2,1)}, bf16[16,4,32,128]{3,2,1,0:T(8,128)(2,1)}) custom-call(bf16[16,4,32,128]{3,2,1,0:T(8,128)(2,1)} %volume.1, bf16[16,4,32,128]{3,2,1,0:T(8,128)(2,1)} %cotangent.1, bf16[27,32,128]{2,1,0:T(8,128)(2,1)} %bitcast.2, f32[1,32]{1,0:T(1,128)} %bitcast.3), custom_call_target="tpu_custom_call" | custom-call | flops 3623878656 | bytes 2097152 | tf_op jit(solution)/shard_map/pallas_call | solution.py:346
  40.5 0.0 copy-start
  40.5 1.9 %copy.8 = bf16[16,4,32,128]{3,2,1,0:T(8,128)(2,1)} copy(bf16[16,4,32,128]{3,2,1,0:T(8,128)(2,1)} %get-tuple-element.4) | data formatting | bytes 1048576
  42.5 0.0 copy-done
  42.5 0.8 %copy.9 = bf16[16,4,32,128]{3,2,1,0:T(8,128)(2,1)} copy(bf16[16,4,32,128]{3,2,1,0:T(8,128)(2,1)S(1)} %copy-done) | data formatting | bytes 1048576
Async XLA Ops:
  40.5 2.0 %copy-start = (bf16[16,4,32,128]{3,2,1,0:T(8,128)(2,1)S(1)}, bf16[16,4,32,128]{3,2,1,0:T(8,128)(2,1)}, u32[]{:S(2)}) copy-start(bf16[16,4,32,128]{3,2,1,0:T(8,128)(2,1)} %get-tuple-element.5) | copy-start | bytes 1572868
